TPU v7x, 128 devices: a whole 4x4x4 slice. The times are simulated.
128 devices in a mesh: ty: 8 (over x, core), tx: 16 (over z, y).
Axes of the slice: x: 4, y: 4, z: 4, core: 2. Of those that a mesh axis runs over, the one named last changes fastest.
Arguments:
- beam_depth: float32 [8192, 512], P(('ty', 'tx')), may hold values from -6 to 6
- backscatter: float32 [8192, 512], P(('ty', 'tx')), may hold values from -6 to 6
- grazing: float32 [8192, 512], P(('ty', 'tx')), may hold values from -6 to 6
- quality: float32 [8192, 512], P(('ty', 'tx')), may hold values from 0.25 to 2
- beam_valid: int32 [8192, 512], P(('ty', 'tx')), may hold values 0 or 1
- beam_row: int32 [8192, 512], P(('ty', 'tx')), may hold values from 0 to 63
- beam_col: int32 [8192, 512], P(('ty', 'tx')), may hold values from 0 to 63
- tidal_zone: int32 [8192], P(('ty', 'tx')), may hold values from 0 to 63
- ping_tile: int32 [8192], P(('ty', 'tx')), may hold values from 0 to 127, as said below
- tide_offsets: float32 [64], replicated, may hold values from -1 to 1
Outputs:
- gridded: float32 [8, 512, 1024], P(None, 'ty', 'tx')
Inputs may be any that keep to these rules, and one draw needn't show every extreme that they name: `ping_tile`: tile t is the tile in row t // 16 and column t % 16. In each aligned block of 64 pings no tile is named more than 2 times, and one tile is named exactly 2 times in every block.
All inputs are finite; a program needn't handle non-finite values. No bound on the sum of `beam_valid` on one device may be relied on, other than what follows from the above.
Results may differ from a plain program's by a relative error of at most 0.000073.
Values sent between devices are 32-bit elements; how exact they have to be, the bound alone decides.
No kernel may reach another device: no remote copies, remote signals or barrier semaphores. Data moves between devices by JAX's collectives and lax.ppermute only.
A program may use at most 64 MiB of HBM per device.

v0:
```python
import functools
import math

import jax
import jax.numpy as jnp
from jax import lax
from jax.experimental import pallas as pl
from jax.experimental.pallas import tpu as pltpu
from jax.sharding import PartitionSpec as P

F32 = jnp.float32
BF16 = jnp.bfloat16
BEAMS = 512
CHANNELS = 8
MARGIN = 7
TILE = 64
FIELDS = 5
LANES = 128
GROUPS = BEAMS // LANES
RANKS = 2
BATCH = 32
TAIL = 8
SIGMA = 2.5
VMEM = pltpu.CompilerParams(vmem_limit_bytes=40 * 2**20)

_profile = [math.exp(-j * j / (2 * SIGMA * SIGMA)) for j in range(-MARGIN, MARGIN + 1)]
TAPS = [value / sum(_profile) for value in _profile]


def vmem():
    return pl.BlockSpec(memory_space=pltpu.VMEM)


def pack_kernel(tile_h, zone_h, tide_h, depth_h, back_h, graz_h, quality_h, valid_h, row_h, col_h, out,
                tile, zone, tide, depth, back, graz, quality, valid, row, col, cell, ready, blank, seen,
                sems, blank_sem, sent):
    pings = depth.shape[0]
    copies = [
        pltpu.make_async_copy(source, target, sems.at[i])
        for i, (source, target) in enumerate(
            (
                (tile_h, tile),
                (zone_h, zone),
                (tide_h, tide),
                (quality_h, quality),
                (valid_h, valid),
                (row_h, row),
                (col_h, col),
                (depth_h, depth),
                (back_h, back),
                (graz_h, graz),
            )
        )
    ]
    for copy in copies:
        copy.start()

    def empty(i, _):
        blank[i] = jnp.full((GROUPS, LANES), -1.0, F32)
        return 0

    lax.fori_loop(0, blank.shape[0], empty, 0, unroll=8)
    blanks = pltpu.make_async_copy(blank, out.at[:, FIELDS - 1], blank_sem)
    blanks.start()

    def clear(i, _):
        seen[i] = 0
        return 0

    lax.fori_loop(0, seen.shape[0], clear, 0, unroll=8)
    for copy in copies:
        copy.wait()
    quality[...] = quality[...] * valid[...].astype(F32)
    cell[...] = (row[...] * TILE + col[...]).astype(F32)
    blanks.wait()

    def place(p, _):
        target = tile[p]
        rank = seen[target]
        seen[target] = rank + 1
        down, across = lax.shift_right_logical(target, 4), target & 15
        chip = lax.shift_right_logical(down, 1) * 16 + across
        slot = chip * 4 + (down & 1) * 2 + rank
        offset = tide[zone[p]]
        here = pl.ds(p, 1)
        for f, field in enumerate((depth, back, graz, quality, cell)):
            values = offset - field[here, :] if f == 0 else field[here, :]
            for j in range(GROUPS):
                ready[p, f, pl.ds(j, 1), :] = values[:, j * LANES : (j + 1) * LANES]
        pltpu.make_async_copy(ready.at[p], out.at[slot], sent).start()
        return 0

    lax.fori_loop(0, pings, place, 0, unroll=8)
    pltpu.make_async_copy(ready, out.at[pl.ds(0, pings)], sent).wait()


def both(rows):
    return jnp.concatenate([rows, rows], 0).astype(BF16)


def factors(x, slot, spots):
    sub = lax.broadcasted_iota(jnp.int32, (8, LANES), 0)
    zero = jnp.zeros((16, LANES), BF16)
    one = jnp.ones((16, LANES), BF16)
    left, right = [], []
    for j in range(GROUPS):
        height, back, graz, weight, cell = (
            jnp.broadcast_to(x[slot, f, pl.ds(j, 1), :], (8, LANES)) for f in range(FIELDS)
        )
        first = jnp.where(
            (sub == 1) | (sub == 2) | (sub == 5),
            height,
            jnp.where((sub == 3) | (sub == 4), back, jnp.where(sub >= 6, graz, 1.0)),
        )
        second = jnp.where(
            sub == 2,
            height,
            jnp.where((sub == 4) | (sub == 5), back, jnp.where(sub == 7, graz, 1.0)),
        )
        stats = weight * first * second
        high = stats.astype(BF16).astype(F32)
        halves = jnp.concatenate([high, stats - high], 0).astype(BF16)
        coarse = jnp.floor(cell * (1.0 / 256.0))
        fine = both(cell - 256.0 * coarse)
        coarse = both(coarse)
        left.append(
            jnp.concatenate(
                [jnp.where(coarse == jnp.asarray(r, BF16), halves, zero) for r in range(16)], 0
            )
        )
        right.append(jnp.concatenate([jnp.where(fine == s, one, zero) for s in spots], 0))
    return jnp.concatenate(left, 1), jnp.concatenate(right, 1)


def deposit_kernel(x, mine, mates, acc, part, heads, table_v, table, sem):
    slots = x.shape[0]
    core = lax.axis_index("ty") % 2

    def head(s, _):
        heads[pl.ds(s, 1), :] = x[s, FIELDS - 1, pl.ds(0, 1), :]
        return 0

    lax.fori_loop(0, slots, head, 0, unroll=16)
    lane = lax.broadcasted_iota(jnp.int32, (8, slots), 1)
    pick = jnp.where(lax.broadcasted_iota(jnp.int32, (8, LANES), 1) == 0, 1.0, 0.0)
    filled = jnp.where(heads[...] >= 0.0, 1.0, 0.0)
    full = lax.dot_general(
        pick.astype(BF16), filled.astype(BF16), (((1,), (1,)), ((), ())),
        preferred_element_type=F32,
    )
    i = lax.broadcasted_iota(jnp.int32, (slots, slots), 0)
    j = lax.broadcasted_iota(jnp.int32, (slots, slots), 1)
    before = jnp.where((i < j) & ((i & 2) == (j & 2)), 1.0, 0.0).astype(BF16)
    position = jnp.dot(full.astype(BF16), before, preferred_element_type=F32)
    numbers = jnp.concatenate([lane.astype(F32), jnp.ones((8, slots), F32)], 0).astype(BF16)
    wanted = i.astype(F32)
    for side in range(2):
        ours = (lane & 2) == 2 * side
        key = jnp.where(ours & (full > 0.0), position, -1.0)
        match = jnp.where(jnp.broadcast_to(key[0:1], (slots, slots)) == wanted, 1.0, 0.0)
        found = lax.dot_general(
            numbers, match.astype(BF16), (((1,), (1,)), ((), ())), preferred_element_type=F32
        )
        gap = jnp.max(
            jnp.where(ours & (full == 0.0), lane.astype(F32), -1.0), axis=1, keepdims=True
        )
        count = jnp.sum(found[8:], axis=1, keepdims=True)
        listed = found[:8] + (1.0 - found[8:]) * gap
        table_v[side] = jnp.where(lane == slots - 1, count, listed).astype(jnp.int32)
    copy = pltpu.make_async_copy(table_v, table, sem)
    copy.start()
    acc[...] = jnp.zeros_like(acc)
    base = lax.broadcasted_iota(jnp.int32, (16, LANES), 0)
    spots = [(base + 16 * k).astype(F32).astype(BF16) for k in range(16)]
    copy.wait()
    counts = [table[side, 0, slots - 1] for side in range(2)]

    def add(first, side, size):
        pairs = [factors(x, table[side, 0, first + u], spots) for u in range(size)]
        left = jnp.concatenate([a for a, _ in pairs], 1)
        right = jnp.concatenate([b for _, b in pairs], 1)
        total = lax.dot_general(
            left, right, (((1,), (1,)), ((), ())), preferred_element_type=F32
        )
        acc[side, 0] += total[:, :LANES]
        acc[side, 1] += total[:, LANES:]

    whole = [(count + TAIL - 1) // BATCH for count in counts]
    rest = [
        (jnp.maximum(count - BATCH * n, 0) + TAIL - 1) // TAIL for count, n in zip(counts, whole)
    ]

    def step(t, _):
        side = (t >= whole[0]).astype(jnp.int32)
        add((t - side * whole[0]) * BATCH, side, BATCH)
        return 0

    def tail(t, _):
        side = (t >= rest[0]).astype(jnp.int32)
        start = jnp.where(side > 0, whole[1], whole[0]) * BATCH
        add(start + (t - side * rest[0]) * TAIL, side, TAIL)
        return 0

    lax.fori_loop(0, whole[0] + whole[1], step, 0)
    lax.fori_loop(0, rest[0] + rest[1], tail, 0)
    for side in range(2):
        for ch in range(CHANNELS):
            for piece in range(2):
                rows = acc[side, piece, pl.ds(ch, 16, stride=16), :]
                rows += acc[side, piece, pl.ds(ch + 8, 16, stride=16), :]
                for q in range(2):
                    part[ch, pl.ds(TILE * side + 2 * piece + q, 16, stride=4), 0:TILE] = rows[
                        :, q * TILE : (q + 1) * TILE
                    ]
    own = pl.ds(pl.multiple_of(core * (TILE - 8), 8), TILE + 8)
    other = pl.ds(pl.multiple_of((1 - core) * (TILE - 8), 8), TILE + 8)
    for ch in range(CHANNELS):
        mine[ch] = part[ch, own, 0:TILE]
        mates[ch] = part[ch, other, 0:TILE]


def join_kernel(mine, mates, total, rim):
    core = lax.axis_index("ty") % 2
    for ch in range(CHANNELS):
        total[ch] = mine[ch] + mates[ch]
        rim[ch] = total[ch, pl.ds(pl.multiple_of(core * TILE, 8), 8), :]


def smoothed(ext, ch):
    total = None
    for j in range(2 * MARGIN + 1):
        term = TAPS[j] * ext[ch, pl.ds(1 + j, TILE), :]
        total = term if total is None else total + term
    return total


def rows_kernel(window, rim, out, near, far, ext):
    place = lax.axis_index("ty")
    core = place % 2
    beyond = (place == 0) | (place == lax.axis_size("ty") - 1)
    odd = lax.axis_index("tx") % 2
    inside = pl.ds(pl.multiple_of(8 - core * 8, 8), TILE + 8)
    outside = pl.ds(pl.multiple_of(core * (TILE + 8), 8), 8)
    for ch in range(CHANNELS):
        ext[ch, inside, :] = window[ch]
        ext[ch, outside, :] = jnp.where(beyond, 0.0, rim[ch])
    for ch in range(CHANNELS):
        out[ch] = smoothed(ext, ch).T
        near[ch] = out[ch, pl.ds(pl.multiple_of((1 - odd) * (TILE - 8), 8), 8), :]
        far[ch] = out[ch, pl.ds(pl.multiple_of(odd * (TILE - 8), 8), 8), :]


def inner_kernel(own, out, ext):
    for ch in range(CHANNELS):
        ext[ch, 0:8, :] = jnp.zeros((8, TILE), F32)
        ext[ch, 8 : 8 + TILE, :] = own[ch]
        ext[ch, 8 + TILE : 16 + TILE, :] = jnp.zeros((8, TILE), F32)
    for ch in range(CHANNELS):
        out[ch] = smoothed(ext, ch)


def columns_kernel(own, inner, near, far, out, ext):
    place = lax.axis_index("tx")
    odd = place % 2
    beyond = (place == 0) | (place == lax.axis_size("tx") - 1)
    near_rows = pl.ds(pl.multiple_of((1 - odd) * 40, 8), 8)
    far_rows = pl.ds(pl.multiple_of(odd * 40, 8), 8)
    for ch in range(CHANNELS):
        ext[ch, 8:24, :] = own[ch, 0:16]
        ext[ch, 24:40, :] = own[ch, TILE - 16 : TILE]
        ext[ch, near_rows, :] = near[ch]
        ext[ch, far_rows, :] = jnp.where(beyond, 0.0, far[ch])
    scale = None
    for ch in range(CHANNELS):
        ends = []
        for first in (1, 25):
            total = None
            for j in range(2 * MARGIN + 1):
                term = TAPS[j] * ext[ch, pl.ds(first + j, 8), :]
                total = term if total is None else total + term
            ends.append(total)
        total = jnp.concatenate([ends[0], inner[ch, 8 : TILE - 8], ends[1]], 0)
        if ch == 0:
            scale = 1.0 + total
        out[ch] = (total / scale).T


def swap(x, axis, first):
    count = lax.axis_size(axis)
    pairs = [(i, (i + 1) % count) for i in range(first, count, 2)]
    return lax.ppermute(x, axis, pairs + [(b, a) for a, b in pairs])


def shards(depth, back, graz, quality, valid, row, col, zone, tile, tide):
    down, across = lax.axis_size("ty"), lax.axis_size("tx")
    slots = down * across * RANKS
    pings = depth.shape[0]
    shape = jax.ShapeDtypeStruct
    hbm = pl.BlockSpec(memory_space=pltpu.HBM)
    block = (pings, BEAMS)
    packed = pl.pallas_call(
        pack_kernel,
        out_shape=shape((slots, FIELDS, GROUPS, LANES), F32),
        in_specs=[hbm] * 10,
        out_specs=hbm,
        scratch_shapes=[
            pltpu.SMEM((pings,), jnp.int32),
            pltpu.SMEM((pings,), jnp.int32),
            pltpu.SMEM(tide.shape, F32),
        ]
        + [pltpu.VMEM(block, F32)] * 4
        + [pltpu.VMEM(block, jnp.int32)] * 3
        + [
            pltpu.VMEM(block, F32),
            pltpu.VMEM((pings, FIELDS, GROUPS, LANES), F32),
            pltpu.VMEM((slots, GROUPS, LANES), F32),
            pltpu.SMEM((down * across,), jnp.int32),
            pltpu.SemaphoreType.DMA((10,)),
            pltpu.SemaphoreType.DMA,
            pltpu.SemaphoreType.DMA,
        ],
        compiler_params=pltpu.CompilerParams(vmem_limit_bytes=60 * 2**20),
        name="pack",
    )(tile, zone, tide, depth, back, graz, quality, valid, row, col)
    groups = [
        [(2 * chip + core) * across + i for chip in range(down // 2) for i in range(across)]
        for core in range(2)
    ]
    arrived = lax.all_to_all(
        packed, ("ty", "tx"), split_axis=0, concat_axis=0, tiled=True, axis_index_groups=groups
    )
    window = shape((CHANNELS, TILE + 8, TILE), F32)
    rim = shape((CHANNELS, 8, TILE), F32)
    ext = pltpu.VMEM((CHANNELS, TILE + 16, TILE), F32)
    mine, mates = pl.pallas_call(
        deposit_kernel,
        out_shape=(window, window),
        in_specs=[vmem()],
        out_specs=(vmem(),) * 2,
        scratch_shapes=[
            pltpu.VMEM((2, 2, 256, LANES), F32),
            pltpu.VMEM((CHANNELS, 2 * TILE, LANES), F32),
            pltpu.VMEM((slots, LANES), F32),
            pltpu.VMEM((2, 8, slots), jnp.int32),
            pltpu.SMEM((2, 8, slots), jnp.int32),
            pltpu.SemaphoreType.DMA,
        ],
        compiler_params=VMEM,
        name="deposit",
    )(arrived)
    total, edge = pl.pallas_call(
        join_kernel,
        out_shape=(window, rim),
        in_specs=[vmem()] * 2,
        out_specs=(vmem(),) * 2,
        compiler_params=VMEM,
        name="join",
    )(mine, swap(mates, "ty", 0))
    rows, near, far = pl.pallas_call(
        rows_kernel,
        out_shape=(shape((CHANNELS, TILE, TILE), F32), rim, rim),
        in_specs=[vmem()] * 2,
        out_specs=(vmem(),) * 3,
        scratch_shapes=[ext],
        compiler_params=VMEM,
        name="rows",
    )(total, swap(edge, "ty", 1))
    near, far = swap(near, "tx", 0), swap(far, "tx", 1)
    inner = pl.pallas_call(
        inner_kernel,
        out_shape=shape((CHANNELS, TILE, TILE), F32),
        in_specs=[vmem()],
        out_specs=vmem(),
        scratch_shapes=[ext],
        compiler_params=VMEM,
        cost_estimate=pl.CostEstimate(flops=10**7, bytes_accessed=10**6, transcendentals=0),
        name="inner",
    )(rows)
    return pl.pallas_call(
        columns_kernel,
        out_shape=shape((CHANNELS, TILE, TILE), F32),
        in_specs=[vmem()] * 4,
        out_specs=vmem(),
        scratch_shapes=[pltpu.VMEM((CHANNELS, 48, TILE), F32)],
        compiler_params=VMEM,
        name="columns",
    )(rows, inner, near, far)


def solution(mesh):
    pings = P(("ty", "tx"))
    return jax.shard_map(
        shards,
        mesh=mesh,
        in_specs=(pings,) * 9 + (P(),),
        out_specs=P(None, "ty", "tx"),
        check_vma=False,
    )
```

profile of v0, /device:TPU:0, one launch (start us, length us, event | category | flops | bytes accessed | tf_op | source)
XLA Modules:
  0.0 73.9 jit_solution(9276289788688075002)
XLA Ops:
  0.0 2.8 %pack.1 = f32[256,5,4,128]{3,2,1,0:T(4,128)} custom-call(s32[64]{0:T(128)} %tile_h.1, s32[64]{0:T(128)} %zone_h.1, f32[64]{0:T(128)} %tide_h.1, f32[64,512]{1,0:T(8,128)} %depth_h.1, f32[64,512]{1,0:T(8,128)} %back_h.1, f32[64,512]{1,0:T(8,128)} %graz_h.1, f32[64,512]{1,0:T(8,128)} %quality_h.1, s32[64,512]{1,0:T(8,128)} %valid_h.1, s32[64,512]{1,0:T(8,128)} %row_h.1, ...), custom_call_target="tpu_custom_call" | custom-call | tf_op jit(solution)/shard_map/pack/pallas_call | solution.py:301
  2.9 47.1 %all_to_all.5.x = f32[256,5,4,128]{3,2,1,0:T(4,128)S(1)} all-to-all(f32[256,5,4,128]{3,2,1,0:T(4,128)} %pack.1), channel_id=1, replica_groups={{0,1,2,3,4,5,6,7,8,9,10,11,12,13,14,15,32,33,34,35,36,37,38,39,40,41,42..., dimensions={0} | all-to-all | bytes 5242880 | tf_op jit(solution)/shard_map/all_to_all | solution.py:329
  49.9 8.9 %deposit.1 = (f32[8,72,64]{2,1,0:T(8,128)S(1)}, f32[8,72,64]{2,1,0:T(8,128)S(1)}) custom-call(f32[256,5,4,128]{3,2,1,0:T(4,128)S(1)} %all_to_all.5.x), custom_call_target="tpu_custom_call" | custom-call | tf_op jit(solution)/shard_map/deposit/pallas_call | solution.py:335
  58.8 0.1 collective-permute-start
  58.9 1.6 %collective-permute-done.mates = f32[8,72,64]{2,1,0:T(8,128)S(1)} collective-permute-done((f32[8,72,64]{2,1,0:T(8,128)S(1)}, f32[8,72,64]{2,1,0:T(8,128)S(1)}, u32[]{:S(2)}, u32[]{:S(2)}) %collective-permute-start) | collective-permute-done | bytes 147488 | tf_op jit(solution)/shard_map/ppermute | solution.py:291
  60.5 0.1 collective-permute-start.1
  60.6 4.5 %collective-permute-done.1.rim = f32[8,8,64]{2,1,0:T(8,128)S(1)} collective-permute-done((f32[8,8,64]{2,1,0:T(8,128)S(1)}, f32[8,8,64]{2,1,0:T(8,128)S(1)}, u32[]{:S(2)}, u32[]{:S(2)}) %collective-permute-start.1) | collective-permute-done | bytes 16416 | tf_op jit(solution)/shard_map/ppermute | solution.py:291
  65.1 0.4 rows.1
  65.6 0.1 collective-permute-start.2
  65.7 0.1 collective-permute-start.3
  65.8 0.3 inner.1
  66.1 3.5 %collective-permute-done.2.near = f32[8,8,64]{2,1,0:T(8,128)S(1)} collective-permute-done((f32[8,8,64]{2,1,0:T(8,128)S(1)}, f32[8,8,64]{2,1,0:T(8,128)S(1)}, u32[]{:S(2)}, u32[]{:S(2)}) %collective-permute-start.2) | collective-permute-done | bytes 16416 | tf_op jit(solution)/shard_map/ppermute | solution.py:291
  69.6 3.4 %collective-permute-done.3.far = f32[8,8,64]{2,1,0:T(8,128)S(1)} collective-permute-done((f32[8,8,64]{2,1,0:T(8,128)S(1)}, f32[8,8,64]{2,1,0:T(8,128)S(1)}, u32[]{:S(2)}, u32[]{:S(2)}) %collective-permute-start.3) | collective-permute-done | bytes 16416 | tf_op jit(solution)/shard_map/ppermute | solution.py:291
  73.0 0.9 %columns.1 = f32[8,64,64]{2,1,0:T(8,128)} custom-call(f32[8,64,64]{2,1,0:T(8,128)S(1)} %get-tuple-element.16.own, f32[8,64,64]{2,1,0:T(8,128)S(1)} %inner.1, f32[8,8,64]{2,1,0:T(8,128)S(1)} %collective-permute-done.2.near, f32[8,8,64]{2,1,0:T(8,128)S(1)} %collective-permute-done.3.far), custom_call_target="tpu_custom_call" | custom-call | tf_op jit(solution)/shard_map/columns/pallas_call | solution.py:379
  (1 shorter events, 0.0 us)
Async XLA Ops:
  58.8 1.7 %collective-permute-start = (f32[8,72,64]{2,1,0:T(8,128)S(1)}, f32[8,72,64]{2,1,0:T(8,128)S(1)}, u32[]{:S(2)}, u32[]{:S(2)}) collective-permute-start(f32[8,72,64]{2,1,0:T(8,128)S(1)} %get-tuple-element.13), channel_id=1, source_target_pairs={{0,16},{32,48},{64,80},{96,112},{16,0},{48,32},{80,64},{112,96},{1... | collective-permute-start | bytes 442376 | tf_op jit(solution)/shard_map/ppermute | solution.py:291
  60.5 4.6 %collective-permute-start.1 = (f32[8,8,64]{2,1,0:T(8,128)S(1)}, f32[8,8,64]{2,1,0:T(8,128)S(1)}, u32[]{:S(2)}, u32[]{:S(2)}) collective-permute-start(f32[8,8,64]{2,1,0:T(8,128)S(1)} %get-tuple-element.15), channel_id=1, source_target_pairs={{16,32},{48,64},{80,96},{112,0},{32,16},{64,48},{96,80},{0,112},{1... | collective-permute-start | bytes 49160 | tf_op jit(solution)/shard_map/ppermute | solution.py:291
  65.6 4.0 %collective-permute-start.2 = (f32[8,8,64]{2,1,0:T(8,128)S(1)}, f32[8,8,64]{2,1,0:T(8,128)S(1)}, u32[]{:S(2)}, u32[]{:S(2)}) collective-permute-start(f32[8,8,64]{2,1,0:T(8,128)S(1)} %get-tuple-element.17), channel_id=1, source_target_pairs={{0,1},{2,3},{4,5},{6,7},{8,9},{10,11},{12,13},{14,15},{1,0},{3,2},... | collective-permute-start | bytes 49160 | tf_op jit(solution)/shard_map/ppermute | solution.py:291
  65.7 7.3 %collective-permute-start.3 = (f32[8,8,64]{2,1,0:T(8,128)S(1)}, f32[8,8,64]{2,1,0:T(8,128)S(1)}, u32[]{:S(2)}, u32[]{:S(2)}) collective-permute-start(f32[8,8,64]{2,1,0:T(8,128)S(1)} %get-tuple-element.18), channel_id=1, source_target_pairs={{1,2},{3,4},{5,6},{7,8},{9,10},{11,12},{13,14},{15,0},{2,1},{4,3},... | collective-permute-start | bytes 49160 | tf_op jit(solution)/shard_map/ppermute | solution.py:291
where the time goes:
time: 74.2 us; the launch traced here: 73.9 us
  blocking collectives  47.1 us (63%)
  Pallas kernels  13.4 us (18%)
  waiting for transfers between devices  13 us (18%)
    all_to_all x1, blocking collectives, shards(): lax.all_to_all(packed, ('ty', 'tx'), split_axis=0, concat_axis=0, tiled=T...  47.1 us
    ppermute x4, waiting for transfers between devices, swap(): return lax.ppermute(x, axis, pairs + [(b, a) for a, b in pairs])  13 us
    pallas_call x1, Pallas kernels, shards(): pl.pallas_call(deposit_kernel, out_shape=(window, window), in_specs=[vmem...  8.86 us
    pallas_call x1, Pallas kernels, shards(): pl.pallas_call(pack_kernel, out_shape=shape((slots, FIELDS, GROUPS, LANES...  2.84 us
  transfers between devices with their start and end apart: 4, of which 4 were waited for; matrix products, arithmetic and copies ran while one was open for 0% of the time, Pallas kernels for 0%

commit v1 on v0

--- a/solution.py
+++ b/solution.py
@@ -32,8 +32,7 @@
 
 
 def pack_kernel(tile_h, zone_h, tide_h, depth_h, back_h, graz_h, quality_h, valid_h, row_h, col_h, out,
-                tile, zone, tide, depth, back, graz, quality, valid, row, col, cell, ready, blank, seen,
-                sems, blank_sem, sent):
+                tile, zone, tide, depth, back, graz, quality, valid, row, col, cell, seen, sems):
     pings = depth.shape[0]
     copies = [
         pltpu.make_async_copy(source, target, sems.at[i])
@@ -56,12 +55,10 @@
         copy.start()
 
     def empty(i, _):
-        blank[i] = jnp.full((GROUPS, LANES), -1.0, F32)
-        return 0
-
-    lax.fori_loop(0, blank.shape[0], empty, 0, unroll=8)
-    blanks = pltpu.make_async_copy(blank, out.at[:, FIELDS - 1], blank_sem)
-    blanks.start()
+        out[i, FIELDS - 1] = jnp.full((GROUPS, LANES), -1.0, F32)
+        return 0
+
+    lax.fori_loop(0, out.shape[0], empty, 0, unroll=8)
 
     def clear(i, _):
         seen[i] = 0
@@ -72,7 +69,6 @@
         copy.wait()
     quality[...] = quality[...] * valid[...].astype(F32)
     cell[...] = (row[...] * TILE + col[...]).astype(F32)
-    blanks.wait()
 
     def place(p, _):
         target = tile[p]
@@ -86,12 +82,10 @@
         for f, field in enumerate((depth, back, graz, quality, cell)):
             values = offset - field[here, :] if f == 0 else field[here, :]
             for j in range(GROUPS):
-                ready[p, f, pl.ds(j, 1), :] = values[:, j * LANES : (j + 1) * LANES]
-        pltpu.make_async_copy(ready.at[p], out.at[slot], sent).start()
+                out[slot, f, pl.ds(j, 1), :] = values[:, j * LANES : (j + 1) * LANES]
         return 0
 
     lax.fori_loop(0, pings, place, 0, unroll=8)
-    pltpu.make_async_copy(ready, out.at[pl.ds(0, pings)], sent).wait()
 
 
 def both(rows):
@@ -300,9 +294,9 @@
     block = (pings, BEAMS)
     packed = pl.pallas_call(
         pack_kernel,
-        out_shape=shape((slots, FIELDS, GROUPS, LANES), F32),
+        out_shape=pltpu.VMEM((slots, FIELDS, GROUPS, LANES), F32),
         in_specs=[hbm] * 10,
-        out_specs=hbm,
+        out_specs=vmem(),
         scratch_shapes=[
             pltpu.SMEM((pings,), jnp.int32),
             pltpu.SMEM((pings,), jnp.int32),
@@ -312,12 +306,8 @@
         + [pltpu.VMEM(block, jnp.int32)] * 3
         + [
             pltpu.VMEM(block, F32),
-            pltpu.VMEM((pings, FIELDS, GROUPS, LANES), F32),
-            pltpu.VMEM((slots, GROUPS, LANES), F32),
             pltpu.SMEM((down * across,), jnp.int32),
             pltpu.SemaphoreType.DMA((10,)),
-            pltpu.SemaphoreType.DMA,
-            pltpu.SemaphoreType.DMA,
         ],
         compiler_params=pltpu.CompilerParams(vmem_limit_bytes=60 * 2**20),
         name="pack",

time: 74.2 us -> 73.2 us (0.987); the launches traced: 73.9 us -> 72 us
  Pallas kernels: 13.4 us -> 10.4 us
  starting transfers between devices: 0.33 us -> 2.81 us
  waiting for transfers between devices: 13 us -> 11.9 us
    ppermute x4, starting transfers between devices: 0.33 us -> 2.81 us  [swap(): return lax.ppermute(x, axis, pairs + [(b, a) for a, b in pairs])]
    pallas_call x1, Pallas kernels: 8.86 us -> 6.59 us  [shards(): pl.pallas_call(deposit_kernel, out_shape=(window, window), in_specs=[vmem...]
    ppermute x4, waiting for transfers between devices: 13 us -> 11.9 us  [swap(): return lax.ppermute(x, axis, pairs + [(b, a) for a, b in pairs])]
where the time goes in v1:
time: 73.2 us; the launch traced here: 72 us
  blocking collectives  46.9 us (64%)
  waiting for transfers between devices  11.9 us (16%)
  Pallas kernels  10.4 us (14%)
  starting transfers between devices  2.81 us (4%)
    all_to_all x1, blocking collectives, shards(): lax.all_to_all(packed, ('ty', 'tx'), split_axis=0, concat_axis=0, tiled=T...  46.9 us
    ppermute x4, waiting for transfers between devices, swap(): return lax.ppermute(x, axis, pairs + [(b, a) for a, b in pairs])  11.9 us
    pallas_call x1, Pallas kernels, shards(): pl.pallas_call(deposit_kernel, out_shape=(window, window), in_specs=[vmem...  6.59 us
    ppermute x4, starting transfers between devices, swap(): return lax.ppermute(x, axis, pairs + [(b, a) for a, b in pairs])  2.81 us
    pallas_call x1, Pallas kernels, shards(): pl.pallas_call(pack_kernel, out_shape=pltpu.VMEM((slots, FIELDS, GROUPS,...  2.18 us
  transfers between devices with their start and end apart: 4, of which 4 were waited for; matrix products, arithmetic and copies ran while one was open for 0% of the time, Pallas kernels for 0%

profile of v1, /device:TPU:0, one launch (start us, length us, event | category | flops | bytes accessed | tf_op | source)
XLA Modules:
  0.0 72.0 jit_solution(4020511825353286966)
XLA Ops:
  0.0 2.2 %pack.1 = f32[256,5,4,128]{3,2,1,0:T(4,128)S(1)} custom-call(s32[64]{0:T(128)} %tile_h.1, s32[64]{0:T(128)} %zone_h.1, f32[64]{0:T(128)} %tide_h.1, f32[64,512]{1,0:T(8,128)} %depth_h.1, f32[64,512]{1,0:T(8,128)} %back_h.1, f32[64,512]{1,0:T(8,128)} %graz_h.1, f32[64,512]{1,0:T(8,128)} %quality_h.1, s32[64,512]{1,0:T(8,128)} %valid_h.1, s32[64,512]{1,0:T(8,128)} %row_h.1, ...), custom_call_target="tpu_custom_call" | custom-call | tf_op jit(solution)/shard_map/pack/pallas_call | solution.py:295
  2.2 46.9 %all_to_all.5.x = f32[256,5,4,128]{3,2,1,0:T(4,128)S(1)} all-to-all(f32[256,5,4,128]{3,2,1,0:T(4,128)S(1)} %pack.1), channel_id=1, replica_groups={{0,1,2,3,4,5,6,7,8,9,10,11,12,13,14,15,32,33,34,35,36,37,38,39,40,41,42..., dimensions={0} | all-to-all | bytes 5242880 | tf_op jit(solution)/shard_map/all_to_all | solution.py:319
  49.1 6.6 %deposit.1 = (f32[8,72,64]{2,1,0:T(8,128)S(1)}, f32[8,72,64]{2,1,0:T(8,128)S(1)}) custom-call(f32[256,5,4,128]{3,2,1,0:T(4,128)S(1)} %all_to_all.5.x), custom_call_target="tpu_custom_call" | custom-call | tf_op jit(solution)/shard_map/deposit/pallas_call | solution.py:325
  55.6 0.1 collective-permute-start
  55.7 1.6 %collective-permute-done.mates = f32[8,72,64]{2,1,0:T(8,128)S(1)} collective-permute-done((f32[8,72,64]{2,1,0:T(8,128)S(1)}, f32[8,72,64]{2,1,0:T(8,128)S(1)}, u32[]{:S(2)}, u32[]{:S(2)}) %collective-permute-start) | collective-permute-done | bytes 147488 | tf_op jit(solution)/shard_map/ppermute | solution.py:285
  57.4 0.7 %collective-permute-start.1 = (f32[8,8,64]{2,1,0:T(8,128)S(1)}, f32[8,8,64]{2,1,0:T(8,128)S(1)}, u32[]{:S(2)}, u32[]{:S(2)}) collective-permute-start(f32[8,8,64]{2,1,0:T(8,128)S(1)} %get-tuple-element.15), channel_id=1, source_target_pairs={{16,32},{48,64},{80,96},{112,0},{32,16},{64,48},{96,80},{0,112},{1... | collective-permute-start | bytes 49160 | tf_op jit(solution)/shard_map/ppermute | solution.py:285
  58.1 3.9 %collective-permute-done.1.rim = f32[8,8,64]{2,1,0:T(8,128)S(1)} collective-permute-done((f32[8,8,64]{2,1,0:T(8,128)S(1)}, f32[8,8,64]{2,1,0:T(8,128)S(1)}, u32[]{:S(2)}, u32[]{:S(2)}) %collective-permute-start.1) | collective-permute-done | bytes 16416 | tf_op jit(solution)/shard_map/ppermute | solution.py:285
  62.0 0.4 rows.1
  62.4 1.5 %collective-permute-start.2 = (f32[8,8,64]{2,1,0:T(8,128)S(1)}, f32[8,8,64]{2,1,0:T(8,128)S(1)}, u32[]{:S(2)}, u32[]{:S(2)}) collective-permute-start(f32[8,8,64]{2,1,0:T(8,128)S(1)} %get-tuple-element.17), channel_id=1, source_target_pairs={{0,1},{2,3},{4,5},{6,7},{8,9},{10,11},{12,13},{14,15},{1,0},{3,2},... | collective-permute-start | bytes 49160 | tf_op jit(solution)/shard_map/ppermute | solution.py:285
  63.9 0.5 collective-permute-start.3
  64.4 0.3 inner.1
  64.7 1.7 %collective-permute-done.2.near = f32[8,8,64]{2,1,0:T(8,128)S(1)} collective-permute-done((f32[8,8,64]{2,1,0:T(8,128)S(1)}, f32[8,8,64]{2,1,0:T(8,128)S(1)}, u32[]{:S(2)}, u32[]{:S(2)}) %collective-permute-start.2) | collective-permute-done | bytes 16416 | tf_op jit(solution)/shard_map/ppermute | solution.py:285
  66.4 4.7 %collective-permute-done.3.far = f32[8,8,64]{2,1,0:T(8,128)S(1)} collective-permute-done((f32[8,8,64]{2,1,0:T(8,128)S(1)}, f32[8,8,64]{2,1,0:T(8,128)S(1)}, u32[]{:S(2)}, u32[]{:S(2)}) %collective-permute-start.3) | collective-permute-done | bytes 16416 | tf_op jit(solution)/shard_map/ppermute | solution.py:285
  71.2 0.9 %columns.1 = f32[8,64,64]{2,1,0:T(8,128)} custom-call(f32[8,64,64]{2,1,0:T(8,128)S(1)} %get-tuple-element.16.own, f32[8,64,64]{2,1,0:T(8,128)S(1)} %inner.1, f32[8,8,64]{2,1,0:T(8,128)S(1)} %collective-permute-done.2.near, f32[8,8,64]{2,1,0:T(8,128)S(1)} %collective-permute-done.3.far), custom_call_target="tpu_custom_call" | custom-call | tf_op jit(solution)/shard_map/columns/pallas_call | solution.py:369
  (1 shorter events, 0.0 us)
Async XLA Ops:
  55.6 1.7 %collective-permute-start = (f32[8,72,64]{2,1,0:T(8,128)S(1)}, f32[8,72,64]{2,1,0:T(8,128)S(1)}, u32[]{:S(2)}, u32[]{:S(2)}) collective-permute-start(f32[8,72,64]{2,1,0:T(8,128)S(1)} %get-tuple-element.13), channel_id=1, source_target_pairs={{0,16},{32,48},{64,80},{96,112},{16,0},{48,32},{80,64},{112,96},{1... | collective-permute-start | bytes 442376 | tf_op jit(solution)/shard_map/ppermute | solution.py:285
  57.4 4.6 %collective-permute-start.1 = (f32[8,8,64]{2,1,0:T(8,128)S(1)}, f32[8,8,64]{2,1,0:T(8,128)S(1)}, u32[]{:S(2)}, u32[]{:S(2)}) collective-permute-start(f32[8,8,64]{2,1,0:T(8,128)S(1)} %get-tuple-element.15), channel_id=1, source_target_pairs={{16,32},{48,64},{80,96},{112,0},{32,16},{64,48},{96,80},{0,112},{1... | collective-permute-start | bytes 49160 | tf_op jit(solution)/shard_map/ppermute | solution.py:285
  62.4 4.0 %collective-permute-start.2 = (f32[8,8,64]{2,1,0:T(8,128)S(1)}, f32[8,8,64]{2,1,0:T(8,128)S(1)}, u32[]{:S(2)}, u32[]{:S(2)}) collective-permute-start(f32[8,8,64]{2,1,0:T(8,128)S(1)} %get-tuple-element.17), channel_id=1, source_target_pairs={{0,1},{2,3},{4,5},{6,7},{8,9},{10,11},{12,13},{14,15},{1,0},{3,2},... | collective-permute-start | bytes 49160 | tf_op jit(solution)/shard_map/ppermute | solution.py:285
  63.9 7.2 %collective-permute-start.3 = (f32[8,8,64]{2,1,0:T(8,128)S(1)}, f32[8,8,64]{2,1,0:T(8,128)S(1)}, u32[]{:S(2)}, u32[]{:S(2)}) collective-permute-start(f32[8,8,64]{2,1,0:T(8,128)S(1)} %get-tuple-element.18), channel_id=1, source_target_pairs={{1,2},{3,4},{5,6},{7,8},{9,10},{11,12},{13,14},{15,0},{2,1},{4,3},... | collective-permute-start | bytes 49160 | tf_op jit(solution)/shard_map/ppermute | solution.py:285

commit v2 on v1

--- a/solution.py
+++ b/solution.py
@@ -160,17 +160,17 @@
         )
         count = jnp.sum(found[8:], axis=1, keepdims=True)
         listed = found[:8] + (1.0 - found[8:]) * gap
-        table_v[side] = jnp.where(lane == slots - 1, count, listed).astype(jnp.int32)
-    copy = pltpu.make_async_copy(table_v, table, sem)
+        table_v[side : side + 1] = jnp.where(lane == slots - 1, count, listed)[0:1].astype(jnp.int32)
+    copy = pltpu.make_async_copy(table_v.at[0:2], table, sem)
     copy.start()
     acc[...] = jnp.zeros_like(acc)
     base = lax.broadcasted_iota(jnp.int32, (16, LANES), 0)
     spots = [(base + 16 * k).astype(F32).astype(BF16) for k in range(16)]
     copy.wait()
-    counts = [table[side, 0, slots - 1] for side in range(2)]
+    counts = [table[side, slots - 1] for side in range(2)]
 
     def add(first, side, size):
-        pairs = [factors(x, table[side, 0, first + u], spots) for u in range(size)]
+        pairs = [factors(x, table[side, first + u], spots) for u in range(size)]
         left = jnp.concatenate([a for a, _ in pairs], 1)
         right = jnp.concatenate([b for _, b in pairs], 1)
         total = lax.dot_general(
@@ -331,8 +331,8 @@
             pltpu.VMEM((2, 2, 256, LANES), F32),
             pltpu.VMEM((CHANNELS, 2 * TILE, LANES), F32),
             pltpu.VMEM((slots, LANES), F32),
-            pltpu.VMEM((2, 8, slots), jnp.int32),
-            pltpu.SMEM((2, 8, slots), jnp.int32),
+            pltpu.VMEM((8, slots), jnp.int32),
+            pltpu.SMEM((2, slots), jnp.int32),
             pltpu.SemaphoreType.DMA,
         ],
         compiler_params=VMEM,

time: 73.2 us -> 72.4 us (0.989); the launches traced: 72 us -> 72.6 us
  starting transfers between devices: 2.81 us -> 4.42 us
  waiting for transfers between devices: 11.9 us -> 11.1 us
    ppermute x4, starting transfers between devices: 2.81 us -> 4.42 us  [swap(): return lax.ppermute(x, axis, pairs + [(b, a) for a, b in pairs])]
    ppermute x4, waiting for transfers between devices: 11.9 us -> 11.1 us  [swap(): return lax.ppermute(x, axis, pairs + [(b, a) for a, b in pairs])]
where the time goes in v2:
time: 72.4 us; the launch traced here: 72.6 us
  blocking collectives  46.9 us (65%)
  waiting for transfers between devices  11.1 us (15%)
  Pallas kernels  10.2 us (14%)
  starting transfers between devices  4.42 us (6%)
    all_to_all x1, blocking collectives, shards(): lax.all_to_all(packed, ('ty', 'tx'), split_axis=0, concat_axis=0, tiled=T...  46.9 us
    ppermute x4, waiting for transfers between devices, swap(): return lax.ppermute(x, axis, pairs + [(b, a) for a, b in pairs])  11.1 us
    pallas_call x1, Pallas kernels, shards(): pl.pallas_call(deposit_kernel, out_shape=(window, window), in_specs=[vmem...  6.36 us
    ppermute x4, starting transfers between devices, swap(): return lax.ppermute(x, axis, pairs + [(b, a) for a, b in pairs])  4.42 us
    pallas_call x1, Pallas kernels, shards(): pl.pallas_call(pack_kernel, out_shape=pltpu.VMEM((slots, FIELDS, GROUPS,...  2.18 us
  transfers between devices with their start and end apart: 4, of which 4 were waited for; matrix products, arithmetic and copies ran while one was open for 0% of the time, Pallas kernels for 0%

profile of v2, /device:TPU:0, one launch (start us, length us, event | category | flops | bytes accessed | tf_op | source)
XLA Modules:
  0.0 72.6 jit_solution(8656417934500177673)
XLA Ops:
  0.0 2.2 %pack.1 = f32[256,5,4,128]{3,2,1,0:T(4,128)S(1)} custom-call(s32[64]{0:T(128)} %tile_h.1, s32[64]{0:T(128)} %zone_h.1, f32[64]{0:T(128)} %tide_h.1, f32[64,512]{1,0:T(8,128)} %depth_h.1, f32[64,512]{1,0:T(8,128)} %back_h.1, f32[64,512]{1,0:T(8,128)} %graz_h.1, f32[64,512]{1,0:T(8,128)} %quality_h.1, s32[64,512]{1,0:T(8,128)} %valid_h.1, s32[64,512]{1,0:T(8,128)} %row_h.1, ...), custom_call_target="tpu_custom_call" | custom-call | tf_op jit(solution)/shard_map/pack/pallas_call | solution.py:295
  2.2 46.9 %all_to_all.5.x = f32[256,5,4,128]{3,2,1,0:T(4,128)S(1)} all-to-all(f32[256,5,4,128]{3,2,1,0:T(4,128)S(1)} %pack.1), channel_id=1, replica_groups={{0,1,2,3,4,5,6,7,8,9,10,11,12,13,14,15,32,33,34,35,36,37,38,39,40,41,42..., dimensions={0} | all-to-all | bytes 5242880 | tf_op jit(solution)/shard_map/all_to_all | solution.py:319
  49.1 6.4 %deposit.1 = (f32[8,72,64]{2,1,0:T(8,128)S(1)}, f32[8,72,64]{2,1,0:T(8,128)S(1)}) custom-call(f32[256,5,4,128]{3,2,1,0:T(4,128)S(1)} %all_to_all.5.x), custom_call_target="tpu_custom_call" | custom-call | tf_op jit(solution)/shard_map/deposit/pallas_call | solution.py:325
  55.4 0.1 collective-permute-start
  55.5 1.6 %collective-permute-done.mates = f32[8,72,64]{2,1,0:T(8,128)S(1)} collective-permute-done((f32[8,72,64]{2,1,0:T(8,128)S(1)}, f32[8,72,64]{2,1,0:T(8,128)S(1)}, u32[]{:S(2)}, u32[]{:S(2)}) %collective-permute-start) | collective-permute-done | bytes 147488 | tf_op jit(solution)/shard_map/ppermute | solution.py:285
  57.1 1.6 %collective-permute-start.1 = (f32[8,8,64]{2,1,0:T(8,128)S(1)}, f32[8,8,64]{2,1,0:T(8,128)S(1)}, u32[]{:S(2)}, u32[]{:S(2)}) collective-permute-start(f32[8,8,64]{2,1,0:T(8,128)S(1)} %get-tuple-element.15), channel_id=1, source_target_pairs={{16,32},{48,64},{80,96},{112,0},{32,16},{64,48},{96,80},{0,112},{1... | collective-permute-start | bytes 49160 | tf_op jit(solution)/shard_map/ppermute | solution.py:285
  58.7 3.0 %collective-permute-done.1.rim = f32[8,8,64]{2,1,0:T(8,128)S(1)} collective-permute-done((f32[8,8,64]{2,1,0:T(8,128)S(1)}, f32[8,8,64]{2,1,0:T(8,128)S(1)}, u32[]{:S(2)}, u32[]{:S(2)}) %collective-permute-start.1) | collective-permute-done | bytes 16416 | tf_op jit(solution)/shard_map/ppermute | solution.py:285
  61.8 0.4 rows.1
  62.2 2.2 %collective-permute-start.2 = (f32[8,8,64]{2,1,0:T(8,128)S(1)}, f32[8,8,64]{2,1,0:T(8,128)S(1)}, u32[]{:S(2)}, u32[]{:S(2)}) collective-permute-start(f32[8,8,64]{2,1,0:T(8,128)S(1)} %get-tuple-element.17), channel_id=1, source_target_pairs={{0,1},{2,3},{4,5},{6,7},{8,9},{10,11},{12,13},{14,15},{1,0},{3,2},... | collective-permute-start | bytes 49160 | tf_op jit(solution)/shard_map/ppermute | solution.py:285
  64.5 0.5 collective-permute-start.3
  65.0 0.3 inner.1
  65.2 1.1 %collective-permute-done.2.near = f32[8,8,64]{2,1,0:T(8,128)S(1)} collective-permute-done((f32[8,8,64]{2,1,0:T(8,128)S(1)}, f32[8,8,64]{2,1,0:T(8,128)S(1)}, u32[]{:S(2)}, u32[]{:S(2)}) %collective-permute-start.2) | collective-permute-done | bytes 16416 | tf_op jit(solution)/shard_map/ppermute | solution.py:285
  66.3 5.3 %collective-permute-done.3.far = f32[8,8,64]{2,1,0:T(8,128)S(1)} collective-permute-done((f32[8,8,64]{2,1,0:T(8,128)S(1)}, f32[8,8,64]{2,1,0:T(8,128)S(1)}, u32[]{:S(2)}, u32[]{:S(2)}) %collective-permute-start.3) | collective-permute-done | bytes 16416 | tf_op jit(solution)/shard_map/ppermute | solution.py:285
  71.7 0.9 %columns.1 = f32[8,64,64]{2,1,0:T(8,128)} custom-call(f32[8,64,64]{2,1,0:T(8,128)S(1)} %get-tuple-element.16.own, f32[8,64,64]{2,1,0:T(8,128)S(1)} %inner.1, f32[8,8,64]{2,1,0:T(8,128)S(1)} %collective-permute-done.2.near, f32[8,8,64]{2,1,0:T(8,128)S(1)} %collective-permute-done.3.far), custom_call_target="tpu_custom_call" | custom-call | tf_op jit(solution)/shard_map/columns/pallas_call | solution.py:369
  (1 shorter events, 0.0 us)
Async XLA Ops:
  55.4 1.7 %collective-permute-start = (f32[8,72,64]{2,1,0:T(8,128)S(1)}, f32[8,72,64]{2,1,0:T(8,128)S(1)}, u32[]{:S(2)}, u32[]{:S(2)}) collective-permute-start(f32[8,72,64]{2,1,0:T(8,128)S(1)} %get-tuple-element.13), channel_id=1, source_target_pairs={{0,16},{32,48},{64,80},{96,112},{16,0},{48,32},{80,64},{112,96},{1... | collective-permute-start | bytes 442376 | tf_op jit(solution)/shard_map/ppermute | solution.py:285
  57.1 4.6 %collective-permute-start.1 = (f32[8,8,64]{2,1,0:T(8,128)S(1)}, f32[8,8,64]{2,1,0:T(8,128)S(1)}, u32[]{:S(2)}, u32[]{:S(2)}) collective-permute-start(f32[8,8,64]{2,1,0:T(8,128)S(1)} %get-tuple-element.15), channel_id=1, source_target_pairs={{16,32},{48,64},{80,96},{112,0},{32,16},{64,48},{96,80},{0,112},{1... | collective-permute-start | bytes 49160 | tf_op jit(solution)/shard_map/ppermute | solution.py:285
  62.2 4.1 %collective-permute-start.2 = (f32[8,8,64]{2,1,0:T(8,128)S(1)}, f32[8,8,64]{2,1,0:T(8,128)S(1)}, u32[]{:S(2)}, u32[]{:S(2)}) collective-permute-start(f32[8,8,64]{2,1,0:T(8,128)S(1)} %get-tuple-element.17), channel_id=1, source_target_pairs={{0,1},{2,3},{4,5},{6,7},{8,9},{10,11},{12,13},{14,15},{1,0},{3,2},... | collective-permute-start | bytes 49160 | tf_op jit(solution)/shard_map/ppermute | solution.py:285
  64.5 7.2 %collective-permute-start.3 = (f32[8,8,64]{2,1,0:T(8,128)S(1)}, f32[8,8,64]{2,1,0:T(8,128)S(1)}, u32[]{:S(2)}, u32[]{:S(2)}) collective-permute-start(f32[8,8,64]{2,1,0:T(8,128)S(1)} %get-tuple-element.18), channel_id=1, source_target_pairs={{1,2},{3,4},{5,6},{7,8},{9,10},{11,12},{13,14},{15,0},{2,1},{4,3},... | collective-permute-start | bytes 49160 | tf_op jit(solution)/shard_map/ppermute | solution.py:285
